TPU v7x, 128 devices: a whole 4x4x4 slice. The times are simulated.
128 devices in a mesh: dp: 4 (over x), rows: 2 (over core), vocab: 16 (over z, y).
Axes of the slice: x: 4, y: 4, z: 4, core: 2. Of those that a mesh axis runs over, the one named last changes fastest.
Arguments:
- hidden: bfloat16 [1024, 8192], P('vocab', ('dp', 'rows')), may hold values from -150 to 150
- head: bfloat16 [8192, 65536], P(('dp', 'rows'), 'vocab'), may hold values from -0.0625 to 0.0625
- ref_logits: bfloat16 [1024, 65536], P(('dp', 'rows'), 'vocab'), may hold values from -200 to 200
- token_ids: int32 [1024], replicated, may hold values from 0 to 65535
- group_ids: int32 [1024], replicated, may hold values from 0 to 63
- response_mask: int32 [1024], replicated, may hold values 0 or 1
- advantages: float32 [64], replicated, may hold values from -4 to 4
Outputs:
- hidden_grad: float32 [1024, 8192], P('vocab', ('dp', 'rows'))
- head_grad: float32 [8192, 65536], P(('dp', 'rows'), 'vocab')
All inputs are finite; a program needn't handle non-finite values.
Results may differ from a plain program's by a relative error of at most 0.0031.
Values may be sent and summed in bfloat16 or wider, within the bound.
A program may use at most 128 MiB of HBM per device.

v0:
```python
import jax
import jax.numpy as jnp
from jax import lax
from jax.sharding import PartitionSpec as P


def sums_given(logits, refs, top, qtop):
    expo = jnp.exp(logits - top[:, None])
    return (
        jnp.sum(expo, axis=1),
        jnp.sum(expo * logits, axis=1),
        jnp.sum(expo * refs, axis=1),
        jnp.sum(jnp.exp(refs - qtop[:, None]), axis=1),
    )


def stats_rows(logits, refs):
    top, qtop = lax.pmax((jnp.max(logits, axis=1), jnp.max(refs, axis=1)), "vocab")
    total, sum_z, sum_r, qtotal = lax.psum(sums_given(logits, refs, top, qtop), "vocab")
    return (top, total, sum_z, sum_r, qtop, qtotal)


def logit_grad(logits, refs, stats, token_sel, group_sel, mask_sel, advantages, first_col):
    top, total, sum_z, sum_r, qtop, qtotal = stats
    lse = top + jnp.log(total)
    qlse = qtop + jnp.log(qtotal)
    mean_z = sum_z / total
    mean_r = sum_r / total
    kl_term = (mean_z - mean_r - lse + qlse)[:, None]
    entropy = (lse - mean_z)[:, None]
    log_p = logits - lse[:, None]
    log_q = refs - qlse[:, None]
    probs = jnp.exp(log_p)
    group_range = jnp.arange(advantages.shape[0], dtype=jnp.int32)
    adv = jnp.sum(
        jnp.where(group_sel[:, None] == group_range[None, :], advantages[None, :], 0.0), axis=1
    )[:, None]
    columns = first_col + jnp.arange(logits.shape[1], dtype=jnp.int32)
    pick = (token_sel[:, None] == columns[None, :]).astype(jnp.float32)
    weight = mask_sel.astype(jnp.float32)[:, None]
    grad = weight * (
        adv * (probs - pick)
        + 0.04 * probs * (log_p - log_q - kl_term)
        + 0.02 * probs * (log_p + entropy)
    )
    return grad.astype(jnp.bfloat16)


def per_device(hidden, head, ref_logits, token_ids, group_ids, response_mask, advantages):
    groups = lax.axis_size(("dp", "rows"))
    block = lax.axis_index(("dp", "rows"))
    shard = lax.axis_index("vocab")
    width_dev = head.shape[1]
    whole = lax.all_gather(hidden, "vocab", axis=0, tiled=True)
    total_rows = whole.shape[0]
    own_rows = total_rows // groups
    piece = whole
    logits = lax.psum_scatter(
        jnp.dot(piece, head, preferred_element_type=jnp.float32),
        ("dp", "rows"),
        scatter_dimension=0,
        tiled=True,
    )
    refs = ref_logits.astype(jnp.float32)
    start = block * own_rows
    token_sel = lax.dynamic_slice_in_dim(token_ids, start, own_rows, 0)
    group_sel = lax.dynamic_slice_in_dim(group_ids, start, own_rows, 0)
    mask_sel = lax.dynamic_slice_in_dim(response_mask, start, own_rows, 0)
    stats = stats_rows(logits, refs)
    grad = logit_grad(
        logits, refs, stats, token_sel, group_sel, mask_sel, advantages, shard * width_dev
    )
    full_grad = lax.all_gather(grad, ("dp", "rows"), axis=0, tiled=True)
    head_grad = lax.dot_general(
        whole, full_grad, (((0,), (0,)), ((), ())), preferred_element_type=jnp.float32
    )
    piece = full_grad
    hidden_grad = lax.psum_scatter(
        lax.dot_general(piece, head, (((1,), (1,)), ((), ())), preferred_element_type=jnp.float32),
        "vocab",
        scatter_dimension=0,
        tiled=True,
    )
    return (hidden_grad, head_grad)


def solution(mesh):
    placed = (
        P("vocab", ("dp", "rows")),
        P(("dp", "rows"), "vocab"),
        P(("dp", "rows"), "vocab"),
        P(),
        P(),
        P(),
        P(),
    )
    return jax.shard_map(
        per_device,
        mesh=mesh,
        in_specs=placed,
        out_specs=(P("vocab", ("dp", "rows")), P(("dp", "rows"), "vocab")),
        check_vma=False,
    )
```

profile of v0, /device:TPU:1, one launch (start us, length us, event | category | flops | bytes accessed | tf_op | source)
XLA Modules:
  0.0 392.0 jit_solution(13633314321265273981)
XLA Ops:
  7.2 0.0 all-gather.3.cloned.1.call-start
  7.2 0.7 all-gather.3.cloned.1.call-update
  7.9 0.0 reduce-scatter.3.cloned.1.call-start
  7.9 49.7 %all-gather.3.cloned.1.call-done = bf16[1024,1024]{1,0:T(8,128)(2,1)} async-done(((bf16[64,1024]{1,0:T(8,128)(2,1)}), bf16[1024,1024]{1,0:T(8,128)(2,1)}) %all-gather.3.cloned.1.call-update) | async-done | bytes 2097168 | tf_op jit(solution)/shard_map/all_gather | solution.py:54
  57.6 16.1 %fusion.12 = f32[1024,4096]{1,0:T(8,128)} fusion(bf16[1024,1024]{1,0:T(8,128)(2,1)} %all-gather.3.cloned.1.call-done, bf16[1024,4096]{1,0:T(8,128)(2,1)} %param.8), kind=kOutput, calls=%fused_computation.26 | convolution fusion | flops 8589934592 | bytes 27262976 | tf_op jit(solution)/shard_map/dot_general | solution.py:59
  73.8 0.0 copy-start.1
  73.8 0.0 copy-start.3
  73.8 0.0 reduce-scatter.3.cloned.1.call-update
  73.8 0.0 all-gather.5.cloned.1.call-start
  73.9 0.8 dynamic_slice.11
  74.7 0.8 dynamic_slice.10
  75.5 0.0 copy-done.1
  75.5 0.2 reduce_max.24
  75.7 0.8 dynamic-slice_convert_fusion
  76.4 0.0 copy-done.3
  76.4 0.1 select_reduce_fusion
  76.5 88.9 %reduce-scatter.3.cloned.1.call-done = f32[128,4096]{1,0:T(8,128)} async-done(((f32[1024,4096]{1,0:T(8,128)}), f32[128,4096]{1,0:T(8,128)}) %reduce-scatter.3.cloned.1.call-update) | async-done | bytes 2097168 | tf_op jit(solution)/shard_map/reduce_scatter | solution.py:58
  165.5 0.0 copy-start
  165.5 1.9 reduce_max.23
  167.4 34.0 %all-reduce.1 = (f32[128]{0:T(128)S(1)}, f32[128]{0:T(128)S(1)}) all-reduce(f32[128]{0:T(128)S(1)} %reduce_max.23, bf16[128]{0:T(256)(128)(2,1)S(1)} %reduce_max.24), channel_id=1, replica_groups=mesh['dp'=4,'rows'=2,'vocab'=16] {'vocab'}, use_global_device_ids=true, to_apply=%region_3.0 | all-reduce | flops 256 | bytes 1792 | tf_op jit(solution)/shard_map/pmax | solution.py:18
  201.4 0.0 copy-done
  201.4 1.2 fusion.9
  202.6 28.5 %all-reduce = (f32[128]{0:T(128)S(1)}, f32[128]{0:T(128)S(1)}, f32[128]{0:T(128)S(1)}, f32[128]{0:T(128)S(1)}) all-reduce(f32[128]{0:T(128)S(1)} %get-tuple-element.8, f32[128]{0:T(128)S(1)} %get-tuple-element.7, f32[128]{0:T(128)S(1)} %get-tuple-element.9, ...), channel_id=1, replica_groups=mesh['dp'=4,'rows'=2,'vocab'=16] {'vocab'}, use_global_device_ids=true, to_apply=%region_5.0 | all-reduce | flops 512 | bytes 4096 | tf_op jit(solution)/shard_map/psum | solution.py:19
  231.2 2.7 fusion.8
  233.8 0.0 all-gather.5.cloned.1.call-update
  233.8 0.2 reduce-scatter.5.cloned.1.call-start
  234.1 60.1 %all-gather.5.cloned.1.call-done = bf16[1024,4096]{1,0:T(8,128)(2,1)} async-done(((bf16[128,4096]{1,0:T(8,128)(2,1)}), bf16[1024,4096]{1,0:T(8,128)(2,1)}) %all-gather.5.cloned.1.call-update) | async-done | bytes 8388624 | tf_op jit(solution)/shard_map/all_gather | solution.py:73
  294.2 15.1 %fusion.13 = f32[1024,1024]{1,0:T(8,128)} fusion(bf16[1024,4096]{1,0:T(8,128)(2,1)} %all-gather.5.cloned.1.call-done, bf16[1024,4096]{1,0:T(8,128)(2,1)} %param.8), kind=kOutput, calls=%fused_computation.27 | convolution fusion | flops 8589934592 | bytes 20971520 | tf_op jit(solution)/shard_map/dot_general | solution.py:79
  309.3 0.0 copy-start.2
  309.3 0.0 reduce-scatter.5.cloned.1.call-update
  309.3 1.6 copy-done.2
  310.9 14.6 %convolution_bitcast_fusion = f32[1024,4096]{0,1:T(8,128)} fusion(bf16[1024,4096]{1,0:T(8,128)(2,1)} %all-gather.5.cloned.1.call-done, bf16[1024,1024]{1,0:T(8,128)(2,1)S(1)} %copy-done.2), kind=kOutput, calls=%fused_computation | convolution fusion | flops 8589934592 | bytes 27262976 | tf_op jit(solution)/shard_map/dot_general | solution.py:74
  325.4 17.6 %copy.10 = f32[1024,4096]{1,0:T(8,128)} copy(f32[1024,4096]{0,1:T(8,128)} %convolution_bitcast_fusion) | data formatting | bytes 33554432
  343.0 42.4 %reduce-scatter.5.cloned.1.call-done = f32[64,1024]{1,0:T(8,128)} async-done(((f32[1024,1024]{1,0:T(8,128)}), f32[64,1024]{1,0:T(8,128)}) %reduce-scatter.5.cloned.1.call-update) | async-done | bytes 262160 | tf_op jit(solution)/shard_map/reduce_scatter | solution.py:78
  (3 shorter events, 0.0 us)
Async XLA Ops:
  7.2 50.5 %all-gather.3.cloned.1.call-start = ((), (), s32[]{:S(2)}) async-start(), calls=%async_computation.2 | async-start | bytes 2228224 | tf_op jit(solution)/shard_map/all_gather | solution.py:54
  7.9 157.6 %reduce-scatter.3.cloned.1.call-start = ((), (), s32[]{:S(2)}) async-start(), calls=%async_computation.3 | async-start | bytes 18874368 | tf_op jit(solution)/shard_map/reduce_scatter | solution.py:58
  73.8 1.7 copy-start.1
  73.8 2.7 copy-start.3
  73.8 220.4 %all-gather.5.cloned.1.call-start = ((), (), s32[]{:S(2)}) async-start(), calls=%async_computation.4 | async-start | bytes 9437184 | tf_op jit(solution)/shard_map/all_gather | solution.py:73
  165.5 35.9 %copy-start = (f32[128,4096]{1,0:T(8,128)S(1)}, f32[128,4096]{1,0:T(8,128)}, u32[]{:S(2)}) copy-start(f32[128,4096]{1,0:T(8,128)} %reduce-scatter.3.cloned.1.call-done) | copy-start | bytes 6291460
  233.8 151.6 %reduce-scatter.5.cloned.1.call-start = ((), (), s32[]{:S(2)}) async-start(), calls=%async_computation.5 | async-start | bytes 4456448 | tf_op jit(solution)/shard_map/reduce_scatter | solution.py:78
  309.3 1.6 copy-start.2
Sparse Core Ops, SparseCore 0:
  10.1 47.4 all-gather.2
  73.9 91.4 reduce-scatter.2
  234.0 60.2 all-gather.4
  309.4 75.9 reduce-scatter.4
where the time goes:
time: 393 us; the launch traced here: 392 us
  waiting for transfers between devices  242 us (62%)
  blocking collectives  62.5 us (16%)
  matrix products  45.7 us (12%)
  local copies, waits for them, and re-layouts  20.8 us (5%)
  between operations  13.8 us (4%)
  other arithmetic  6.92 us (2%)
    reduce_scatter x1, waiting for transfers between devices, per_device(): lax.psum_scatter(jnp.dot(piece, head, preferred_element_type=jnp.float32)...  88.9 us
    all_gather x1, waiting for transfers between devices, per_device(): full_grad = lax.all_gather(grad, ('dp', 'rows'), axis=0, tiled=True)  60.1 us
    all_gather x1, waiting for transfers between devices, per_device(): whole = lax.all_gather(hidden, 'vocab', axis=0, tiled=True)  49.7 us
    reduce_scatter x1, waiting for transfers between devices, per_device(): lax.psum_scatter(lax.dot_general(piece, head, (((1,), (1,)), ((), ())), p...  42.4 us
    pmax x1, blocking collectives, stats_rows(): lax.pmax((jnp.max(logits, axis=1), jnp.max(refs, axis=1)), 'vocab')  34 us
    psum x1, blocking collectives, stats_rows(): lax.psum(sums_given(logits, refs, top, qtop), 'vocab')  28.5 us
    unnamed x9, local copies, waits for them, and re-layouts  19.2 us
    dot_general x1, matrix products, per_device(): jnp.dot(piece, head, preferred_element_type=jnp.float32)  16.1 us
  transfers between devices with their start and end apart: 4, of which 4 were waited for; matrix products, arithmetic and copies ran while one was open for 9% of the time, Pallas kernels for 0%

commit v1 on v0

v1 whole, which is shorter than its diff:
```python
import functools

import jax
import jax.numpy as jnp
from jax import lax
from jax.experimental import pallas as pl
from jax.experimental.pallas import tpu as pltpu
from jax.sharding import PartitionSpec as P

MESH = pl.DeviceIdType.MESH
CHUNKS = 4
NX = 4
NY = 4
NZ = 4
ROWS = 16
SUBS = 2
TILE = 2048
MTILE = 1024
PTILE = 512
LANES = 128
UNIT = 32000.0
F32 = jnp.float32
SENDERS = ("core0", "core1", "h1", "h2", "q1", "q2", "s", "g1y", "g1z", "g2", "c", "a")

ORDER = (
    "A0", "B0", "A1", "B1", "M0", "Q0", "M1", "A2", "Q1", "R0", "B2", "R1", "A3", "Q2", "L0", "B3", "Q3",
    "R2", "S0", "L1", "R3", "M2", "T0", "S1", "L2", "Q4", "F0", "T1", "Q5", "L3", "R4", "M3", "S2", "S3",
    "F1", "Q6", "T2", "L4", "R5", "Q7", "C0", "C1", "R6", "S4", "P0", "T3", "L5", "F2", "R7", "L6", "S5",
    "F3", "T4", "S6", "T5", "C2", "L7", "T6", "C3", "U0", "S7", "F4", "P1", "F5", "T7", "V0", "C4", "C5",
    "F6", "U1", "F7", "P2", "C6", "C7", "P3", "U2", "V1", "U3", "V2", "V3",
)


def fold(values):
    return [values[:, j : j + LANES] for j in range(0, values.shape[1], LANES)]


def column(row):
    square = (LANES, LANES)
    same = lax.broadcasted_iota(jnp.int32, square, 0) == lax.broadcasted_iota(jnp.int32, square, 1)
    return jnp.sum(jnp.where(same, jnp.broadcast_to(row, square), 0.0), axis=1, keepdims=True)


def spread(columns):
    rows = columns[0].shape[0]
    lane = lax.broadcasted_iota(jnp.int32, (rows, LANES), 1)
    tile = jnp.zeros((rows, LANES), F32)
    for j, value in enumerate(columns):
        tile = jnp.where(lane == j, value, tile)
    return tile


def merge(tiles):
    get = lambda tile, j: tile[:, j : j + 1]
    top = functools.reduce(jnp.maximum, [get(t, 0) for t in tiles])
    qtop = functools.reduce(jnp.maximum, [get(t, 4) for t in tiles])
    scale = [jnp.exp(get(t, 0) - top) for t in tiles]
    qscale = [jnp.exp(get(t, 4) - qtop) for t in tiles]
    total, sum_z, sum_r = (sum(get(t, j) * s for t, s in zip(tiles, scale)) for j in (1, 2, 3))
    qtotal = sum(get(t, 5) * s for t, s in zip(tiles, qscale))
    return (top, total, sum_z, sum_r, qtop, qtotal)


def kernel(
    hidden_ref, head_ref, refs_ref, token_ref, group_ref, mask_ref, adv_ref,
    hgrad_ref, dl_out, hid_out,
    head, hid, refs, part, crecv, temp, q1s, q1r, q2s, q2r, zbuf, stat_s, stat_r, dl, pg, ra, rsum, rb,
    tok_c, adv_c, wgt_c, send_sem, recv_sem, local_sem,
):
    x = lax.axis_index("dp")
    core = lax.axis_index("rows")
    shard = lax.axis_index("vocab")
    y, z = lax.rem(shard, NY), lax.div(shard, NY)
    width = head.shape[1]
    half = width // 2
    depth = head.shape[0]
    dhalf = depth // 2
    block = 2 * x + core
    ycd, ylo = lax.div(y, 2), lax.rem(y, 2)

    def xof(step):
        return lax.rem(x + step + 2 * NX, NX)

    def yof(step):
        return lax.rem(y + step, NY)

    def zof(step):
        return lax.rem(z + step, NZ)

    def at_core():
        return {"rows": 1 - core}

    def at_x(step):
        return {"dp": xof(step)}

    def at_y(step):
        return {"vocab": z * NY + yof(step)}

    def at_z(step):
        return {"vocab": zof(step) * NY + y}

    numbers = {}

    def number(key):
        if key[1] in ("q1", "q2", "a+", "a-", "a"):
            return numbers.setdefault(key, len(numbers))
        if key[1] == "c":
            return numbers.setdefault((key[0] // SUBS, "c"), len(numbers))
        return numbers.setdefault(key[:2], len(numbers))

    def send(key, src, dst, device):
        name = key[1] + str(key[0] % 2) if key[1] == "core" else key[1]
        n = next(i for i, start in enumerate(SENDERS) if name.startswith(start))
        pltpu.make_async_remote_copy(
            src_ref=src, dst_ref=dst, send_sem=send_sem.at[n], recv_sem=recv_sem.at[number(key)],
            device_id=device, device_id_type=MESH,
        ).start()

    def arrive(key, view):
        pltpu.make_async_copy(view, view, recv_sem.at[number(key)]).wait()

    def sent(name, view):
        pltpu.make_async_copy(view, view, send_sem.at[SENDERS.index(name)]).wait()

    locals_ = []

    def bring(src, dst):
        copy = pltpu.make_async_copy(src, dst, local_sem.at[len(locals_)])
        copy.start()
        locals_.append(copy)
        return copy

    own = [bring(hidden_ref.at[pl.ds(ROWS * k, ROWS)], hid.at[k, ycd, z, ylo]) for k in range(CHUNKS)]
    head_loads = [
        bring(head_ref.at[pl.ds(j * depth // 4, depth // 4)], head.at[pl.ds(j * depth // 4, depth // 4)])
        for j in range(4)
    ]
    refs_load = bring(refs_ref, refs)
    barrier = pltpu.get_barrier_semaphore()
    peers = [at_core(), at_x(1), at_x(-1)] + [at_y(d) for d in (1, 2, 3)] + [at_z(d) for d in (1, 2, 3)]
    for peer in peers:
        pl.semaphore_signal(barrier, inc=1, device_id=peer, device_id_type=MESH)
    pl.semaphore_wait(barrier, len(peers))

    cols0, cols1 = pl.ds(0, dhalf), pl.ds(dhalf, dhalf)
    def own_row(ref):
        values = ref[...].astype(F32)
        at = lax.broadcasted_iota(jnp.int32, values.shape, 0) == block
        return jnp.sum(jnp.where(at, values, 0.0), axis=0, keepdims=True)

    groups = adv_ref.shape[1]
    group_col = column(own_row(group_ref))
    group_at = lax.broadcasted_iota(jnp.int32, (LANES, groups), 1).astype(F32)
    adv_col = jnp.sum(jnp.where(group_col == group_at, adv_ref[...], 0.0), axis=1, keepdims=True)
    tok_c[...] = jnp.broadcast_to(column(own_row(token_ref)), tok_c.shape)
    adv_c[...] = jnp.broadcast_to(adv_col, adv_c.shape)
    wgt_c[...] = jnp.broadcast_to(column(own_row(mask_ref)), wgt_c.shape)

    def own_rows(ref, k, cols):
        at = 4 * ROWS * (k % SUBS) + ROWS * (k // SUBS)
        return ref[pl.ds(at, ROWS), cols].astype(F32)

    def tiles(lo, hi, body, init):
        def step(i, carry):
            return body(pl.multiple_of(i * TILE, TILE), carry)

        return lax.fori_loop(lo // TILE, hi // TILE, step, init)

    def exponent(top):
        return jnp.floor(jnp.log2(jnp.maximum(top, 1e-30))) + 1.0

    def code(values, by):
        return jnp.round(values * by).astype(jnp.int32).astype(jnp.int16)

    def decode(ref, cols, by):
        return ref[:, cols].astype(jnp.int32).astype(F32) * by

    def unit_of(ref, at):
        return jnp.exp2(ref[:, pl.ds(at, LANES)].astype(jnp.int32).astype(F32)[:, 0:1]) * (1.0 / UNIT)

    def local_sum(k, xd, cols):
        c, low = k // SUBS, k % SUBS
        return part[c % 2, core, xd, low, :, cols] + crecv[c, xd, low, :, cols]

    def stage_a(k):
        own[k].wait()
        for d in (1, 3, 2):
            mine = hid.at[k, ycd, z, ylo, :, cols0]
            send((k, "h1y", d), mine, mine, at_y(d))
            mine = hid.at[k, ycd, z, ylo, :, cols1]
            send((k, "h1z", d), mine, mine, at_z(d))

    def stage_b(k):
        arrive((k, "h1y"), dl.at[0, 0, pl.ds(0, 3), 0, :, cols0])
        arrive((k, "h1z"), dl.at[0, 0, pl.ds(0, 3), 0, :, cols0])
        for d in (1, 3, 2):
            mine = hid.at[k, :, z, :, :, cols0]
            send((k, "h2z", d), mine, mine, at_z(d))
            mine = hid.at[k, ycd, :, ylo, :, cols1]
            send((k, "h2y", d), mine, mine, at_y(d))

    def stage_m(k):
        if k == 0:
            for copy in head_loads:
                copy.wait()
        arrive((k, "h2z"), dl.at[0, :, pl.ds(0, 3), :, :, cols0])
        arrive((k, "h2y"), dl.at[0, :, pl.ds(0, 3), :, :, cols0])
        bring(hid.at[k], hid_out.at[k])
        slot = k % 2
        if k >= 2:
            sent("core" + str(slot), part.at[slot, 1 - core])
        span = width // 4
        for g in range(4):
            def step(i, carry):
                cols = pl.ds(pl.multiple_of(g * span + i * MTILE, MTILE), MTILE)
                rows = hid[k].reshape(16 * ROWS, depth)
                out = jnp.dot(rows, head[:, cols], preferred_element_type=F32)
                part[slot, :, :, :, :, cols] = out.reshape(2, NX, SUBS, ROWS, MTILE)
                return carry

            lax.fori_loop(0, span // MTILE, step, 0)
            cols = pl.ds(g * span, span)
            send((k, "core", g), part.at[slot, 1 - core, :, :, :, cols], crecv.at[k, :, :, :, cols], at_core())

    def stage_q(k):
        if k % SUBS == 0:
            arrive((k // SUBS, "core"), crecv.at[k // SUBS])
        xd = xof(2)

        def first(at, top):
            cols = pl.ds(at, TILE)
            value = local_sum(k, xd, cols)
            temp[:, cols] = value
            return functools.reduce(jnp.maximum, fold(jnp.abs(value)), top)

        top = tiles(0, width, first, jnp.zeros((ROWS, LANES), F32))
        power = exponent(jnp.max(top, axis=1, keepdims=True))
        by = jnp.exp2(-power) * UNIT
        for j in range(2):

            def second(at, carry):
                q1s[k, j, :, pl.ds(pl.multiple_of(at - j * half, TILE), TILE)] = code(temp[:, pl.ds(at, TILE)], by)
                return carry

            tiles(j * half, (j + 1) * half, second, 0)
            q1s[k, j, :, pl.ds(half, LANES)] = jnp.broadcast_to(power, (ROWS, LANES)).astype(jnp.int32).astype(jnp.int16)
            send((k, "q1", j), q1s.at[k, j], q1r.at[k, j], at_x(1 if j == 0 else -1))

    def stage_r(k):
        for j in range(2):
            step = 1 if j == 0 else -1
            xd = xof(step)
            arrive((k, "q1", j), q1r.at[k, j])
            unit = unit_of(q1r.at[k, j], half)

            def plain(at, top):
                cols = pl.ds(at, TILE)
                value = local_sum(k, xd, cols)
                temp[:, cols] = value
                return functools.reduce(jnp.maximum, fold(jnp.abs(value)), top)

            def passing(at, top):
                cols = pl.ds(at, TILE)
                value = local_sum(k, xd, cols)
                value += decode(q1r.at[k, j], pl.ds(pl.multiple_of(at - j * half, TILE), TILE), unit)
                temp[:, cols] = value
                return functools.reduce(jnp.maximum, fold(jnp.abs(value)), top)

            top = tiles(j * half, (j + 1) * half, passing, jnp.zeros((ROWS, LANES), F32))
            top = tiles((1 - j) * half, (2 - j) * half, plain, top)
            power = exponent(jnp.max(top, axis=1, keepdims=True))
            by = jnp.exp2(-power) * UNIT

            def second(at, carry):
                cols = pl.ds(at, TILE)
                q2s[k, j, :, cols] = code(temp[:, cols], by)
                return carry

            tiles(0, width, second, 0)
            q2s[k, j, :, pl.ds(width, LANES)] = jnp.broadcast_to(power, (ROWS, LANES)).astype(jnp.int32).astype(jnp.int16)
            send((k, "q2", j), q2s.at[k, j], q2r.at[k, j], at_x(step))

    def stage_l(k):
        if k == 0:
            refs_load.wait()
        units = []
        for j in range(2):
            arrive((k, "q2", j), q2r.at[k, j])
            units.append(unit_of(q2r.at[k, j], width))

        def first(at, carry):
            top, qtop = carry
            cols = pl.ds(at, TILE)
            value = local_sum(k, x, cols)
            for j in range(2):
                value += decode(q2r.at[k, j], cols, units[j])
            zbuf[k, :, cols] = value
            top = functools.reduce(jnp.maximum, fold(value), top)
            qtop = functools.reduce(jnp.maximum, fold(own_rows(refs, k, cols)), qtop)
            return (top, qtop)

        low = jnp.full((ROWS, LANES), -jnp.inf, F32)
        top, qtop = tiles(0, width, first, (low, low))
        top = jnp.max(top, axis=1, keepdims=True)
        qtop = jnp.max(qtop, axis=1, keepdims=True)

        def second(at, carry):
            cols = pl.ds(at, TILE)
            value = zbuf[k, :, cols]
            ref = own_rows(refs, k, cols)
            expo = jnp.exp(value - top)
            adds = (expo, expo * value, expo * ref, jnp.exp(ref - qtop))
            return tuple(sum(fold(a), c) for a, c in zip(adds, carry))

        sums = tiles(0, width, second, (jnp.zeros((ROWS, LANES), F32),) * 4)
        total, sum_z, sum_r, qtotal = (jnp.sum(s, axis=1, keepdims=True) for s in sums)
        stat_s[k, 0] = spread((top, total, sum_z, sum_r, qtop, qtotal))
        for d in (1, 3, 2):
            send((k, "sy", d), stat_s.at[k, 0], stat_r.at[k, 0, d - 1], at_y(d))

    def stage_s(k):
        arrive((k, "sy"), stat_r.at[k, 0])
        stat_s[k, 1] = spread(merge([stat_s[k, 0]] + [stat_r[k, 0, d] for d in range(3)]))
        for d in (1, 3, 2):
            send((k, "sz", d), stat_s.at[k, 1], stat_r.at[k, 1, d - 1], at_z(d))

    def stage_t(k):
        c, low = k // SUBS, k % SUBS
        arrive((k, "sz"), stat_r.at[k, 1])
        top, total, sum_z, sum_r, qtop, qtotal = merge([stat_s[k, 1]] + [stat_r[k, 1, d] for d in range(3)])
        lse = top + jnp.log(total)
        qlse = qtop + jnp.log(qtotal)
        mean_z = sum_z / total
        mean_r = sum_r / total
        kl_term = mean_z - mean_r - lse + qlse
        entropy = lse - mean_z
        one = pl.ds(0, LANES)
        adv = own_rows(adv_c, k, one)[:, 0:1]
        weight = own_rows(wgt_c, k, one)[:, 0:1]
        base = adv + 0.04 * (qlse - lse - kl_term) + 0.02 * (entropy - lse)
        picked = weight * adv
        spot = own_rows(tok_c, k, one)[:, 0:1].astype(jnp.int32) - shard * width

        def body(at, carry):
            cols = pl.ds(at, TILE)
            value = zbuf[k, :, cols]
            ref = own_rows(refs, k, cols)
            grad = (weight * jnp.exp(value - lse)) * (base + 0.06 * value - 0.04 * ref)
            here = lax.broadcasted_iota(jnp.int32, (ROWS, TILE), 1) + at
            grad = grad - jnp.where(here == spot, picked, 0.0)
            dl[c, core, x, low, :, cols] = grad.astype(jnp.bfloat16)
            return carry

        spans = [pl.ds(0, half), pl.ds(half, half)]
        tiles(0, half, body, 0)
        mine = dl.at[c, core, x, low, :, spans[0]]
        send((k, "a+", 0), mine, mine, at_x(1))
        tiles(half, width, body, 0)
        mine = dl.at[c, core, x, low, :, spans[1]]
        send((k, "a-", 1), mine, mine, at_x(-1))
        send((k, "a+", 1), mine, mine, at_x(1))
        mine = dl.at[c, core, x, low, :, spans[0]]
        send((k, "a-", 0), mine, mine, at_x(-1))
        send((k, "c", 0), dl.at[c, core, x, low], dl.at[c, core, x, low], at_core())

    def stage_f(k):
        c, low = k // SUBS, k % SUBS
        left = dl.at[c, core, xof(-1), low, :, pl.ds(0, half)]
        arrive((k, "a+", 0), left)
        send((k, "a", 1), left, left, at_x(1))
        right = dl.at[c, core, xof(1), low, :, pl.ds(half, half)]
        arrive((k, "a-", 1), right)
        send((k, "a", -1), right, right, at_x(-1))

    def stage_c(k):
        c, low = k // SUBS, k % SUBS
        arrive((k, "a+", 1), dl.at[c, core, xof(-1), low, :, pl.ds(half, half)])
        send((k, "c", 1), dl.at[c, core, xof(-1), low], dl.at[c, core, xof(-1), low], at_core())
        arrive((k, "a-", 0), dl.at[c, core, xof(1), low, :, pl.ds(0, half)])
        send((k, "c", 3), dl.at[c, core, xof(1), low], dl.at[c, core, xof(1), low], at_core())
        arrive((k, "a", 1), dl.at[c, core, xof(2), low, :, pl.ds(0, half)])
        arrive((k, "a", -1), dl.at[c, core, xof(2), low, :, pl.ds(half, half)])
        send((k, "c", 2), dl.at[c, core, xof(2), low], dl.at[c, core, xof(2), low], at_core())

    def stage_p(k):
        arrive((SUBS * k, "c"), dl.at[k, 1 - core])
        bring(dl.at[k], dl_out.at[k])

        def step(i, carry):
            at = pl.ds(pl.multiple_of(i * PTILE, PTILE), PTILE)
            rows = dl[k].reshape(16 * ROWS, width)
            out = lax.dot_general(rows, head[at, :], (((1,), (1,)), ((), ())), preferred_element_type=F32)
            pg[k, :, :, :, :, at] = out.reshape(2, NZ, 2, ROWS, PTILE)
            return carry

        lax.fori_loop(0, dhalf // PTILE, step, 0)
        for d in (1, 3, 2):
            yy = yof(d)
            src = pg.at[k, lax.div(yy, 2), :, lax.rem(yy, 2), :, cols0]
            send((k, "g1y", d), src, ra.at[k, 0, d - 1], at_y(d))
        lax.fori_loop(dhalf // PTILE, depth // PTILE, step, 0)
        for d in (1, 3, 2):
            src = pg.at[k, :, zof(d), :, :, cols1]
            send((k, "g1z", d), src, rb.at[k, 0, d - 1], at_z(d))

    def stage_u(k):
        arrive((k, "g1y"), ra.at[k, 0])
        value = pg[k, ycd, :, ylo, :, cols0]
        for d in range(3):
            value += ra[k, 0, d]
        rsum[k, 0] = value
        for d in (1, 3, 2):
            send((k, "g2z", d), rsum.at[k, 0, zof(d)], ra.at[k, 1, d - 1, 0], at_z(d))
        arrive((k, "g1z"), rb.at[k, 0])
        value = pg[k, :, z, :, :, cols1]
        for d in range(3):
            value += rb[k, 0, d]
        rsum[k, 1] = value.reshape(4, ROWS, dhalf)
        for d in (1, 3, 2):
            send((k, "g2y", d), rsum.at[k, 1, yof(d)], ra.at[k, 1, d - 1, 1], at_y(d))

    def stage_v(k):
        rows = pl.ds(ROWS * k, ROWS)
        for j, (name, mine) in enumerate((("g2z", z), ("g2y", y))):
            value = rsum[k, j, mine]
            arrive((k, name), ra.at[k, 1, :, j])
            for d in range(3):
                value += ra[k, 1, d, j]
            hgrad_ref[rows, pl.ds(j * dhalf, dhalf)] = value

    stages = dict(
        A=stage_a, B=stage_b, M=stage_m, Q=stage_q, R=stage_r, L=stage_l, S=stage_s, T=stage_t,
        F=stage_f, C=stage_c, P=stage_p, U=stage_u, V=stage_v,
    )
    for word in ORDER:
        with jax.named_scope("stage_" + word):
            stages[word[0]](int(word[1:]))
    three = pl.ds(0, 3)
    for name, view in (
        ("core0", part.at[0, 1 - core]), ("core1", part.at[1, 1 - core]),
        ("h1", dl.at[0, 0, three, 0]), ("h2", dl.at[three, 0, :, 0]),
        ("q1", q1s), ("q2", q2s), ("s", stat_r), ("g1y", ra.at[:, 0]), ("g1z", rb), ("g2", ra.at[:, 1, :, pl.ds(0, 2)]),
        ("c", dl.at[:, 1 - core]), ("a", dl.at[:, core, three]),
    ):
        sent(name, view)
    for copy in locals_[len(own) + len(head_loads) + 1 :]:
        copy.wait()


def per_device(hidden, head, ref_logits, token_ids, group_ids, response_mask, advantages):
    depth, width = head.shape
    groups = advantages.shape[0]
    dhalf = depth // 2
    bf16, i16 = jnp.bfloat16, jnp.int16
    any_space = pl.BlockSpec(memory_space=pl.ANY)
    in_vmem = pl.BlockSpec(memory_space=pltpu.VMEM)
    hidden_grad, grads, rows = pl.pallas_call(
        kernel,
        out_shape=(
            jax.ShapeDtypeStruct((CHUNKS * ROWS, depth), F32),
            jax.ShapeDtypeStruct((CHUNKS, 2, NX, SUBS, ROWS, width), bf16),
            jax.ShapeDtypeStruct((CHUNKS, 2, NZ, 2, ROWS, depth), bf16),
        ),
        in_specs=[any_space] * 3 + [in_vmem] * 4,
        out_specs=(in_vmem, any_space, any_space),
        scratch_shapes=[
            pltpu.VMEM((depth, width), bf16),
            pltpu.VMEM((CHUNKS, 2, NZ, 2, ROWS, depth), bf16),
            pltpu.VMEM(ref_logits.shape, bf16),
            pltpu.VMEM((2, 2, NX, SUBS, ROWS, width), F32),
            pltpu.VMEM((CHUNKS, NX, SUBS, ROWS, width), F32),
            pltpu.VMEM((ROWS, width), F32),
            pltpu.VMEM((SUBS * CHUNKS, 2, ROWS, width // 2 + LANES), i16),
            pltpu.VMEM((SUBS * CHUNKS, 2, ROWS, width // 2 + LANES), i16),
            pltpu.VMEM((SUBS * CHUNKS, 2, ROWS, width + LANES), i16),
            pltpu.VMEM((SUBS * CHUNKS, 2, ROWS, width + LANES), i16),
            pltpu.VMEM((SUBS * CHUNKS, ROWS, width), F32),
            pltpu.VMEM((SUBS * CHUNKS, 2, ROWS, LANES), F32),
            pltpu.VMEM((SUBS * CHUNKS, 2, 3, ROWS, LANES), F32),
            pltpu.VMEM((CHUNKS, 2, NX, SUBS, ROWS, width), bf16),
            pltpu.VMEM((CHUNKS, 2, NZ, 2, ROWS, depth), F32),
            pltpu.VMEM((CHUNKS, 2, 3, 4, ROWS, dhalf), F32),
            pltpu.VMEM((CHUNKS, 2, 4, ROWS, dhalf), F32),
            pltpu.VMEM((CHUNKS, 1, 3, 2, 2, ROWS, dhalf), F32),
            pltpu.VMEM((LANES, LANES), F32),
            pltpu.VMEM((LANES, LANES), F32),
            pltpu.VMEM((LANES, LANES), F32),
            pltpu.SemaphoreType.DMA((len(SENDERS),)),
            pltpu.SemaphoreType.DMA((34 * CHUNKS,)),
            pltpu.SemaphoreType.DMA((20,)),
        ],
        compiler_params=pltpu.CompilerParams(
            collective_id=0, has_side_effects=True, vmem_limit_bytes=62 * 1024 * 1024
        ),
    )(
        hidden, head, ref_logits,
        token_ids.reshape(8, LANES), group_ids.reshape(8, LANES), response_mask.reshape(8, LANES),
        advantages.reshape(1, groups),
    )
    head_grad = lax.dot_general(
        rows.reshape(-1, depth), grads.reshape(-1, width), (((0,), (0,)), ((), ())), preferred_element_type=F32
    )
    return (hidden_grad, head_grad)


def solution(mesh):
    placed = (
        P("vocab", ("dp", "rows")),
        P(("dp", "rows"), "vocab"),
        P(("dp", "rows"), "vocab"),
        P(),
        P(),
        P(),
        P(),
    )
    return jax.shard_map(
        per_device,
        mesh=mesh,
        in_specs=placed,
        out_specs=(P("vocab", ("dp", "rows")), P(("dp", "rows"), "vocab")),
        check_vma=False,
    )
```

time: 393 us -> 133 us (0.34)
  waiting for transfers between devices: 242 us -> 0 us
  Pallas kernels: 0 us -> 115 us
  blocking collectives: 62.5 us -> 0 us
  matrix products: 45.7 us -> 16.5 us
  local copies, waits for them, and re-layouts: 20.8 us -> 0.71 us
  between operations: 13.8 us -> 0.65 us
  other arithmetic: 6.92 us -> 0 us
    reduce_scatter x2 -> x0, waiting for transfers between devices: 131 us -> none  [the longest x1 88.9 us: per_device(): lax.psum_scatter(jnp.dot(piece, head, preferred_element_type=jnp.float32)...]
    pallas_call x0 -> x1, Pallas kernels: none -> 115 us  [per_device(): pl.pallas_call(kernel, out_shape=(jax.ShapeDtypeStruct((CHUNKS * ROWS, de...]
    all_gather x2 -> x0, waiting for transfers between devices: 110 us -> none  [the longest x1 60.1 us: per_device(): full_grad = lax.all_gather(grad, ('dp', 'rows'), axis=0, tiled=True)]
    pmax x1 -> x0, blocking collectives: 34 us -> none  [stats_rows(): lax.pmax((jnp.max(logits, axis=1), jnp.max(refs, axis=1)), 'vocab')]
    dot_general x3 -> x1, matrix products: 45.7 us -> 16.5 us  [per_device(): lax.dot_general(rows.reshape(-1, depth), grads.reshape(-1, width), (((0,)...]
    psum x1 -> x0, blocking collectives: 28.5 us -> none  [stats_rows(): lax.psum(sums_given(logits, refs, top, qtop), 'vocab')]
    unnamed x9 -> x3, local copies, waits for them, and re-layouts: 19.2 us -> 0.71 us
  transfers between devices with their start and end apart: 4 -> 0, of which waited for: 4 -> 0; matrix products, arithmetic and copies ran while one was open for 9% -> 0% of each run, Pallas kernels for 0% -> 0%
where the time goes in v1:
time: 133 us
  Pallas kernels  115 us (86%)
  matrix products  16.5 us (12%)
    pallas_call x1, Pallas kernels, per_device(): pl.pallas_call(kernel, out_shape=(jax.ShapeDtypeStruct((CHUNKS * ROWS, de...  115 us
    dot_general x1, matrix products, per_device(): lax.dot_general(rows.reshape(-1, depth), grads.reshape(-1, width), (((0,)...  16.5 us

profile of v1, /device:TPU:1, one launch (start us, length us, event | category | flops | bytes accessed | tf_op | source)
XLA Modules:
  0.0 132.7 jit_solution(7537865694169811736)
XLA Ops:
  0.6 114.8 %shard_map.86 = (f32[64,1024]{1,0:T(8,128)}, bf16[4,2,4,2,16,4096]{5,4,3,2,1,0:T(8,128)(2,1)}, bf16[4,2,4,2,16,1024]{5,4,3,2,1,0:T(8,128)(2,1)}) custom-call(bf16[64,1024]{1,0:T(8,128)(2,1)} %hidden_ref.1, bf16[1024,4096]{1,0:T(8,128)(2,1)} %head_ref.1, bf16[128,4096]{1,0:T(8,128)(2,1)} %refs_ref.1, s32[8,128]{1,0:T(8,128)} %bitcast.10, s32[8,128]{1,0:T(8,128)} %bitcast.11, ...), custom_call_target="tpu_custom_call" | custom-call | tf_op jit(solution)/shard_map/pallas_call | solution.py:457
  115.5 0.0 copy-start
  115.5 16.5 %convolution_bitcast_fusion = f32[1024,4096]{1,0:T(8,128)} fusion(bf16[4,2,4,2,16,1024]{5,4,3,2,1,0:T(8,128)(2,1)} %get-tuple-element.6, bf16[4,2,4,2,16,4096]{5,4,3,2,1,0:T(8,128)(2,1)} %get-tuple-element.7), kind=kOutput, calls=%fused_computation | convolution fusion | flops 8589934592 | bytes 27262976 | tf_op jit(solution)/shard_map/dot_general | solution.py:500
  132.0 0.0 copy-done
  132.0 0.7 copy.11
Async XLA Ops:
  115.5 16.5 %copy-start = (f32[64,1024]{1,0:T(8,128)S(1)}, f32[64,1024]{1,0:T(8,128)}, u32[]{:S(2)}) copy-start(f32[64,1024]{1,0:T(8,128)} %get-tuple-element.10) | copy-start | bytes 786436

commit v2 on v1

--- a/solution.py
+++ b/solution.py
@@ -20,6 +20,7 @@
 LANES = 128
 UNIT = 32000.0
 F32 = jnp.float32
+SPANS = (512, 1024, 1024, 1024, 512)
 SENDERS = ("core0", "core1", "h1", "h2", "q1", "q2", "s", "g1y", "g1z", "g2", "c", "a")
 
 ORDER = (
@@ -64,8 +65,8 @@
 def kernel(
     hidden_ref, head_ref, refs_ref, token_ref, group_ref, mask_ref, adv_ref,
     hgrad_ref, dl_out, hid_out,
-    head, hid, refs, part, crecv, temp, q1s, q1r, q2s, q2r, zbuf, stat_s, stat_r, dl, pg, ra, rsum, rb,
-    tok_c, adv_c, wgt_c, send_sem, recv_sem, local_sem,
+    head, hid, refs, part, crecv, temp, q1s, q1r, q2s, q2r, zbuf, stat_s, stat_r, dl, pg, pgs, ga, gb, gc, rsum,
+    tok_c, adv_c, wgt_c, hid_t, send_sem, recv_sem, local_sem,
 ):
     x = lax.axis_index("dp")
     core = lax.axis_index("rows")
@@ -109,7 +110,7 @@
         return numbers.setdefault(key[:2], len(numbers))
 
     def send(key, src, dst, device):
-        name = key[1] + str(key[0] % 2) if key[1] == "core" else key[1]
+        name = key[1] + str(key[0] // SUBS % 2) if key[1] == "core" else key[1]
         n = next(i for i, start in enumerate(SENDERS) if name.startswith(start))
         pltpu.make_async_remote_copy(
             src_ref=src, dst_ref=dst, send_sem=send_sem.at[n], recv_sem=recv_sem.at[number(key)],
@@ -205,26 +206,27 @@
                 copy.wait()
         arrive((k, "h2z"), dl.at[0, :, pl.ds(0, 3), :, :, cols0])
         arrive((k, "h2y"), dl.at[0, :, pl.ds(0, 3), :, :, cols0])
-        bring(hid.at[k], hid_out.at[k])
         slot = k % 2
+        hid_t[:, pl.ds(16 * ROWS * k, 16 * ROWS)] = jnp.swapaxes(hid[k].reshape(16 * ROWS, depth), 0, 1)
+        if k == CHUNKS - 1:
+            bring(hid_t, hid_out)
         if k >= 2:
             sent("core" + str(slot), part.at[slot, 1 - core])
-        span = width // 4
-        for g in range(4):
-            def step(i, carry):
-                cols = pl.ds(pl.multiple_of(g * span + i * MTILE, MTILE), MTILE)
-                rows = hid[k].reshape(16 * ROWS, depth)
+        for lows in ((0,), (1,)) if k == 0 else ((0, 1),):
+            low, many = pl.ds(lows[0], len(lows)), len(lows)
+            for g in range(width // MTILE):
+                cols = pl.ds(g * MTILE, MTILE)
+                rows = hid[k, :, :, low].reshape(8 * many * ROWS, depth)
                 out = jnp.dot(rows, head[:, cols], preferred_element_type=F32)
-                part[slot, :, :, :, :, cols] = out.reshape(2, NX, SUBS, ROWS, MTILE)
-                return carry
-
-            lax.fori_loop(0, span // MTILE, step, 0)
-            cols = pl.ds(g * span, span)
-            send((k, "core", g), part.at[slot, 1 - core, :, :, :, cols], crecv.at[k, :, :, :, cols], at_core())
+                part[slot, :, :, low, :, cols] = out.reshape(2, NX, many, ROWS, MTILE)
+                src = part.at[slot, 1 - core, :, low, :, cols]
+                send((SUBS * k + lows[0], "core", g), src, crecv.at[k, :, low, :, cols], at_core())
 
     def stage_q(k):
-        if k % SUBS == 0:
-            arrive((k // SUBS, "core"), crecv.at[k // SUBS])
+        if k < SUBS:
+            arrive((k, "core"), crecv.at[0, :, k])
+        elif k % SUBS == 0:
+            arrive((k, "core"), crecv.at[k // SUBS])
         xd = xof(2)
 
         def first(at, top):
@@ -391,41 +393,42 @@
             rows = dl[k].reshape(16 * ROWS, width)
             out = lax.dot_general(rows, head[at, :], (((1,), (1,)), ((), ())), preferred_element_type=F32)
             pg[k, :, :, :, :, at] = out.reshape(2, NZ, 2, ROWS, PTILE)
+            pgs[k, :, :, :, :, at] = out.astype(jnp.bfloat16).reshape(2, NZ, 2, ROWS, PTILE)
             return carry
 
         lax.fori_loop(0, dhalf // PTILE, step, 0)
         for d in (1, 3, 2):
             yy = yof(d)
-            src = pg.at[k, lax.div(yy, 2), :, lax.rem(yy, 2), :, cols0]
-            send((k, "g1y", d), src, ra.at[k, 0, d - 1], at_y(d))
+            src = pgs.at[k, lax.div(yy, 2), :, lax.rem(yy, 2), :, cols0]
+            send((k, "g1y", d), src, ga.at[k, d - 1], at_y(d))
         lax.fori_loop(dhalf // PTILE, depth // PTILE, step, 0)
         for d in (1, 3, 2):
-            src = pg.at[k, :, zof(d), :, :, cols1]
-            send((k, "g1z", d), src, rb.at[k, 0, d - 1], at_z(d))
+            src = pgs.at[k, :, zof(d), :, :, cols1]
+            send((k, "g1z", d), src, gb.at[k, d - 1], at_z(d))
 
     def stage_u(k):
-        arrive((k, "g1y"), ra.at[k, 0])
+        arrive((k, "g1y"), ga.at[k])
         value = pg[k, ycd, :, ylo, :, cols0]
         for d in range(3):
-            value += ra[k, 0, d]
+            value += ga[k, d].astype(F32)
         rsum[k, 0] = value
         for d in (1, 3, 2):
-            send((k, "g2z", d), rsum.at[k, 0, zof(d)], ra.at[k, 1, d - 1, 0], at_z(d))
-        arrive((k, "g1z"), rb.at[k, 0])
+            send((k, "g2z", d), rsum.at[k, 0, zof(d)], gc.at[k, d - 1, 0], at_z(d))
+        arrive((k, "g1z"), gb.at[k])
         value = pg[k, :, z, :, :, cols1]
         for d in range(3):
-            value += rb[k, 0, d]
+            value += gb[k, d].astype(F32)
         rsum[k, 1] = value.reshape(4, ROWS, dhalf)
         for d in (1, 3, 2):
-            send((k, "g2y", d), rsum.at[k, 1, yof(d)], ra.at[k, 1, d - 1, 1], at_y(d))
+            send((k, "g2y", d), rsum.at[k, 1, yof(d)], gc.at[k, d - 1, 1], at_y(d))
 
     def stage_v(k):
         rows = pl.ds(ROWS * k, ROWS)
         for j, (name, mine) in enumerate((("g2z", z), ("g2y", y))):
             value = rsum[k, j, mine]
-            arrive((k, name), ra.at[k, 1, :, j])
+            arrive((k, name), gc.at[k, :, j])
             for d in range(3):
-                value += ra[k, 1, d, j]
+                value += gc[k, d, j]
             hgrad_ref[rows, pl.ds(j * dhalf, dhalf)] = value
 
     stages = dict(
@@ -439,12 +442,58 @@
     for name, view in (
         ("core0", part.at[0, 1 - core]), ("core1", part.at[1, 1 - core]),
         ("h1", dl.at[0, 0, three, 0]), ("h2", dl.at[three, 0, :, 0]),
-        ("q1", q1s), ("q2", q2s), ("s", stat_r), ("g1y", ra.at[:, 0]), ("g1z", rb), ("g2", ra.at[:, 1, :, pl.ds(0, 2)]),
+        ("q1", q1s), ("q2", q2s), ("s", stat_r), ("g1y", ga), ("g1z", gb), ("g2", gc),
         ("c", dl.at[:, 1 - core]), ("a", dl.at[:, core, three]),
     ):
         sent(name, view)
     for copy in locals_[len(own) + len(head_loads) + 1 :]:
         copy.wait()
+
+
+def head_kernel(rows_ref, grads_ref, out_ref, rows, grads, outs, row_sem, in_sem, out_sem):
+    starts = [sum(SPANS[:i]) for i in range(len(SPANS))]
+    spans = [pl.ds(at, size) for at, size in zip(starts, SPANS)]
+    loads = [pltpu.make_async_copy(rows_ref, rows, row_sem.at[0])]
+    loads += [
+        pltpu.make_async_copy(grads_ref.at[:, span], grads.at[:, span], in_sem.at[i]) for i, span in enumerate(spans)
+    ]
+    loads[0].start()
+    loads[1].start()
+    loads[2].start()
+    loads[0].wait()
+    stores = []
+    for i, span in enumerate(spans):
+        loads[1 + i].wait()
+        if i + 3 < len(loads):
+            loads[i + 3].start()
+        if i >= 2:
+            stores[i - 2].wait()
+        here = outs.at[i % 2, :, pl.ds(0, SPANS[i])]
+        here[...] = jnp.dot(rows[...], grads[:, span], preferred_element_type=F32)
+        stores.append(pltpu.make_async_copy(here, out_ref.at[:, span], out_sem.at[i]))
+        stores[-1].start()
+    stores[-2].wait()
+    stores[-1].wait()
+
+
+def head_gradient(rows, grads):
+    (depth, tokens), width = rows.shape, grads.shape[1]
+    any_space = pl.BlockSpec(memory_space=pl.ANY)
+    return pl.pallas_call(
+        head_kernel,
+        out_shape=jax.ShapeDtypeStruct((depth, width), F32),
+        in_specs=[any_space] * 2,
+        out_specs=any_space,
+        scratch_shapes=[
+            pltpu.VMEM((depth, tokens), rows.dtype),
+            pltpu.VMEM((tokens, width), grads.dtype),
+            pltpu.VMEM((2, depth, max(SPANS)), F32),
+            pltpu.SemaphoreType.DMA((1,)),
+            pltpu.SemaphoreType.DMA((len(SPANS),)),
+            pltpu.SemaphoreType.DMA((len(SPANS),)),
+        ],
+        compiler_params=pltpu.CompilerParams(vmem_limit_bytes=56 * 1024 * 1024),
+    )(rows, grads)
 
 
 def per_device(hidden, head, ref_logits, token_ids, group_ids, response_mask, advantages):
@@ -459,7 +508,7 @@
         out_shape=(
             jax.ShapeDtypeStruct((CHUNKS * ROWS, depth), F32),
             jax.ShapeDtypeStruct((CHUNKS, 2, NX, SUBS, ROWS, width), bf16),
-            jax.ShapeDtypeStruct((CHUNKS, 2, NZ, 2, ROWS, depth), bf16),
+            jax.ShapeDtypeStruct((depth, 16 * ROWS * CHUNKS), bf16),
         ),
         in_specs=[any_space] * 3 + [in_vmem] * 4,
         out_specs=(in_vmem, any_space, any_space),
@@ -479,14 +528,17 @@
             pltpu.VMEM((SUBS * CHUNKS, 2, 3, ROWS, LANES), F32),
             pltpu.VMEM((CHUNKS, 2, NX, SUBS, ROWS, width), bf16),
             pltpu.VMEM((CHUNKS, 2, NZ, 2, ROWS, depth), F32),
-            pltpu.VMEM((CHUNKS, 2, 3, 4, ROWS, dhalf), F32),
+            pltpu.VMEM((CHUNKS, 2, NZ, 2, ROWS, depth), bf16),
+            pltpu.VMEM((CHUNKS, 3, 4, ROWS, dhalf), bf16),
+            pltpu.VMEM((CHUNKS, 3, 2, 2, ROWS, dhalf), bf16),
+            pltpu.VMEM((CHUNKS, 3, 2, ROWS, dhalf), F32),
             pltpu.VMEM((CHUNKS, 2, 4, ROWS, dhalf), F32),
-            pltpu.VMEM((CHUNKS, 1, 3, 2, 2, ROWS, dhalf), F32),
             pltpu.VMEM((LANES, LANES), F32),
             pltpu.VMEM((LANES, LANES), F32),
             pltpu.VMEM((LANES, LANES), F32),
+            pltpu.VMEM((depth, 16 * ROWS * CHUNKS), bf16),
             pltpu.SemaphoreType.DMA((len(SENDERS),)),
-            pltpu.SemaphoreType.DMA((34 * CHUNKS,)),
+            pltpu.SemaphoreType.DMA((34 * CHUNKS + 1,)),
             pltpu.SemaphoreType.DMA((20,)),
         ],
         compiler_params=pltpu.CompilerParams(
@@ -497,9 +549,7 @@
         token_ids.reshape(8, LANES), group_ids.reshape(8, LANES), response_mask.reshape(8, LANES),
         advantages.reshape(1, groups),
     )
-    head_grad = lax.dot_general(
-        rows.reshape(-1, depth), grads.reshape(-1, width), (((0,), (0,)), ((), ())), preferred_element_type=F32
-    )
+    head_grad = head_gradient(rows, grads.reshape(-1, width))
     return (hidden_grad, head_grad)
 
 

time: 133 us -> 125 us (0.940)
  matrix products: 16.5 us -> 0 us
  Pallas kernels: 115 us -> 124 us
    dot_general x1 -> x0, matrix products: 16.5 us -> none  [per_device(): lax.dot_general(rows.reshape(-1, depth), grads.reshape(-1, width), (((0,)...]
    pallas_call x0 -> x1, Pallas kernels: none -> 13 us  [head_gradient(): pl.pallas_call(head_kernel, out_shape=jax.ShapeDtypeStruct((depth, width)...]
    pallas_call x1, Pallas kernels: 115 us -> 111 us  [per_device(): pl.pallas_call(kernel, out_shape=(jax.ShapeDtypeStruct((CHUNKS * ROWS, de...]
where the time goes in v2:
time: 125 us
  Pallas kernels  124 us (99%)
    pallas_call x1, Pallas kernels, per_device(): pl.pallas_call(kernel, out_shape=(jax.ShapeDtypeStruct((CHUNKS * ROWS, de...  111 us
    pallas_call x1, Pallas kernels, head_gradient(): pl.pallas_call(head_kernel, out_shape=jax.ShapeDtypeStruct((depth, width)...  13 us

profile of v2, /device:TPU:1, one launch (start us, length us, event | category | flops | bytes accessed | tf_op | source)
XLA Modules:
  0.0 125.0 jit_solution(6042393807666332175)
XLA Ops:
  0.6 110.6 %shard_map.86 = (f32[64,1024]{1,0:T(8,128)}, bf16[4,2,4,2,16,4096]{5,4,3,2,1,0:T(8,128)(2,1)}, bf16[1024,1024]{1,0:T(8,128)(2,1)}) custom-call(bf16[64,1024]{1,0:T(8,128)(2,1)} %hidden_ref.1, bf16[1024,4096]{1,0:T(8,128)(2,1)} %head_ref.1, bf16[128,4096]{1,0:T(8,128)(2,1)} %refs_ref.1, s32[8,128]{1,0:T(8,128)} %bitcast.6, s32[8,128]{1,0:T(8,128)} %bitcast.7, ...), custom_call_target="tpu_custom_call" | custom-call | tf_op jit(solution)/shard_map/pallas_call | solution.py:506
  111.3 0.0 copy-start
  111.3 13.0 %shard_map.87 = f32[1024,4096]{1,0:T(8,128)} custom-call(bf16[1024,1024]{1,0:T(8,128)(2,1)} %get-tuple-element.6.rows_ref, bf16[1024,4096]{1,0:T(8,128)(2,1)} %bitcast.5), custom_call_target="tpu_custom_call" | custom-call | tf_op jit(solution)/shard_map/pallas_call | solution.py:482
  124.3 0.0 copy-done
  124.3 0.7 copy.10
Async XLA Ops:
  111.3 13.0 %copy-start = (f32[64,1024]{1,0:T(8,128)S(1)}, f32[64,1024]{1,0:T(8,128)}, u32[]{:S(2)}) copy-start(f32[64,1024]{1,0:T(8,128)} %get-tuple-element.10) | copy-start | bytes 786436

commit v3 on v2

--- a/solution.py
+++ b/solution.py
@@ -20,7 +20,8 @@
 LANES = 128
 UNIT = 32000.0
 F32 = jnp.float32
-SPANS = (512, 1024, 1024, 1024, 512)
+SPANS = (512, 1024, 1024, 512)
+EARLY = 1024
 SENDERS = ("core0", "core1", "h1", "h2", "q1", "q2", "s", "g1y", "g1z", "g2", "c", "a")
 
 ORDER = (
@@ -28,7 +29,7 @@
     "R2", "S0", "L1", "R3", "M2", "T0", "S1", "L2", "Q4", "F0", "T1", "Q5", "L3", "R4", "M3", "S2", "S3",
     "F1", "Q6", "T2", "L4", "R5", "Q7", "C0", "C1", "R6", "S4", "P0", "T3", "L5", "F2", "R7", "L6", "S5",
     "F3", "T4", "S6", "T5", "C2", "L7", "T6", "C3", "U0", "S7", "F4", "P1", "F5", "T7", "V0", "C4", "C5",
-    "F6", "U1", "F7", "P2", "C6", "C7", "P3", "U2", "V1", "U3", "V2", "V3",
+    "F6", "U1", "F7", "P2", "C6", "C7", "P3", "H3", "U2", "V1", "U3", "V2", "V3",
 )
 
 
@@ -64,9 +65,9 @@
 
 def kernel(
     hidden_ref, head_ref, refs_ref, token_ref, group_ref, mask_ref, adv_ref,
-    hgrad_ref, dl_out, hid_out,
+    hgrad_ref, dl_out, hid_out, early_out,
     head, hid, refs, part, crecv, temp, q1s, q1r, q2s, q2r, zbuf, stat_s, stat_r, dl, pg, pgs, ga, gb, gc, rsum,
-    tok_c, adv_c, wgt_c, hid_t, send_sem, recv_sem, local_sem,
+    tok_c, adv_c, wgt_c, hid_t, early, send_sem, recv_sem, local_sem,
 ):
     x = lax.axis_index("dp")
     core = lax.axis_index("rows")
@@ -406,6 +407,11 @@
             src = pgs.at[k, :, zof(d), :, :, cols1]
             send((k, "g1z", d), src, gb.at[k, d - 1], at_z(d))
 
+    def stage_h(k):
+        grads = dl[:, :, :, :, :, pl.ds(width - EARLY, EARLY)].reshape(16 * ROWS * CHUNKS, EARLY)
+        early[...] = jnp.dot(hid_t[...], grads, preferred_element_type=F32)
+        bring(early, early_out)
+
     def stage_u(k):
         arrive((k, "g1y"), ga.at[k])
         value = pg[k, ycd, :, ylo, :, cols0]
@@ -433,7 +439,7 @@
 
     stages = dict(
         A=stage_a, B=stage_b, M=stage_m, Q=stage_q, R=stage_r, L=stage_l, S=stage_s, T=stage_t,
-        F=stage_f, C=stage_c, P=stage_p, U=stage_u, V=stage_v,
+        F=stage_f, C=stage_c, P=stage_p, H=stage_h, U=stage_u, V=stage_v,
     )
     for word in ORDER:
         with jax.named_scope("stage_" + word):
@@ -450,7 +456,9 @@
         copy.wait()
 
 
-def head_kernel(rows_ref, grads_ref, out_ref, rows, grads, outs, row_sem, in_sem, out_sem):
+def head_kernel(
+    rows_ref, grads_ref, early_ref, hidden_ref, hgrad_ref, out_ref, rows, grads, outs, early, hgrad, row_sem, in_sem, out_sem, pass_sem
+):
     starts = [sum(SPANS[:i]) for i in range(len(SPANS))]
     spans = [pl.ds(at, size) for at, size in zip(starts, SPANS)]
     loads = [pltpu.make_async_copy(rows_ref, rows, row_sem.at[0])]
@@ -461,9 +469,24 @@
     loads[1].start()
     loads[2].start()
     loads[0].wait()
+    taken = [
+        pltpu.make_async_copy(early_ref, early, pass_sem.at[0]),
+        pltpu.make_async_copy(hidden_ref, hgrad, pass_sem.at[1]),
+    ]
+    passed = [
+        pltpu.make_async_copy(early, out_ref.at[:, pl.ds(sum(SPANS), EARLY)], pass_sem.at[2]),
+        pltpu.make_async_copy(hgrad, hgrad_ref, pass_sem.at[3]),
+    ]
     stores = []
     for i, span in enumerate(spans):
         loads[1 + i].wait()
+        if i == 0:
+            for copy in taken:
+                copy.start()
+        if i == 1:
+            for copy, last in zip(taken, passed):
+                copy.wait()
+                last.start()
         if i + 3 < len(loads):
             loads[i + 3].start()
         if i >= 2:
@@ -472,28 +495,34 @@
         here[...] = jnp.dot(rows[...], grads[:, span], preferred_element_type=F32)
         stores.append(pltpu.make_async_copy(here, out_ref.at[:, span], out_sem.at[i]))
         stores[-1].start()
-    stores[-2].wait()
-    stores[-1].wait()
-
-
-def head_gradient(rows, grads):
+    for copy in stores[-2:] + passed:
+        copy.wait()
+
+
+def head_gradient(rows, grads, early, hidden_grad):
     (depth, tokens), width = rows.shape, grads.shape[1]
     any_space = pl.BlockSpec(memory_space=pl.ANY)
     return pl.pallas_call(
         head_kernel,
-        out_shape=jax.ShapeDtypeStruct((depth, width), F32),
-        in_specs=[any_space] * 2,
-        out_specs=any_space,
+        out_shape=(
+            jax.ShapeDtypeStruct(hidden_grad.shape, F32),
+            jax.ShapeDtypeStruct((depth, width), F32),
+        ),
+        in_specs=[any_space] * 4,
+        out_specs=(any_space, any_space),
         scratch_shapes=[
             pltpu.VMEM((depth, tokens), rows.dtype),
             pltpu.VMEM((tokens, width), grads.dtype),
             pltpu.VMEM((2, depth, max(SPANS)), F32),
+            pltpu.VMEM((depth, EARLY), F32),
+            pltpu.VMEM(hidden_grad.shape, F32),
             pltpu.SemaphoreType.DMA((1,)),
             pltpu.SemaphoreType.DMA((len(SPANS),)),
             pltpu.SemaphoreType.DMA((len(SPANS),)),
+            pltpu.SemaphoreType.DMA((4,)),
         ],
         compiler_params=pltpu.CompilerParams(vmem_limit_bytes=56 * 1024 * 1024),
-    )(rows, grads)
+    )(rows, grads, early, hidden_grad)
 
 
 def per_device(hidden, head, ref_logits, token_ids, group_ids, response_mask, advantages):
@@ -503,15 +532,16 @@
     bf16, i16 = jnp.bfloat16, jnp.int16
     any_space = pl.BlockSpec(memory_space=pl.ANY)
     in_vmem = pl.BlockSpec(memory_space=pltpu.VMEM)
-    hidden_grad, grads, rows = pl.pallas_call(
+    hidden_grad, grads, rows, early = pl.pallas_call(
         kernel,
         out_shape=(
             jax.ShapeDtypeStruct((CHUNKS * ROWS, depth), F32),
             jax.ShapeDtypeStruct((CHUNKS, 2, NX, SUBS, ROWS, width), bf16),
             jax.ShapeDtypeStruct((depth, 16 * ROWS * CHUNKS), bf16),
+            jax.ShapeDtypeStruct((depth, EARLY), F32),
         ),
         in_specs=[any_space] * 3 + [in_vmem] * 4,
-        out_specs=(in_vmem, any_space, any_space),
+        out_specs=(in_vmem, any_space, any_space, any_space),
         scratch_shapes=[
             pltpu.VMEM((depth, width), bf16),
             pltpu.VMEM((CHUNKS, 2, NZ, 2, ROWS, depth), bf16),
@@ -537,6 +567,7 @@
             pltpu.VMEM((LANES, LANES), F32),
             pltpu.VMEM((LANES, LANES), F32),
             pltpu.VMEM((depth, 16 * ROWS * CHUNKS), bf16),
+            pltpu.VMEM((depth, EARLY), F32),
             pltpu.SemaphoreType.DMA((len(SENDERS),)),
             pltpu.SemaphoreType.DMA((34 * CHUNKS + 1,)),
             pltpu.SemaphoreType.DMA((20,)),
@@ -549,8 +580,7 @@
         token_ids.reshape(8, LANES), group_ids.reshape(8, LANES), response_mask.reshape(8, LANES),
         advantages.reshape(1, groups),
     )
-    head_grad = head_gradient(rows, grads.reshape(-1, width))
-    return (hidden_grad, head_grad)
+    return head_gradient(rows, grads.reshape(-1, width), early, hidden_grad)
 
 
 def solution(mesh):

time: 125 us -> 125 us (level)
  no operation moved by 1% of the time
where the time goes in v3:
time: 125 us
  Pallas kernels  124 us (99%)
    pallas_call x1, Pallas kernels, per_device(): pl.pallas_call(kernel, out_shape=(jax.ShapeDtypeStruct((CHUNKS * ROWS, de...  111 us
    pallas_call x1, Pallas kernels, head_gradient(): pl.pallas_call(head_kernel, out_shape=(jax.ShapeDtypeStruct(hidden_grad.s...  13.2 us

profile of v3, /device:TPU:1, one launch (start us, length us, event | category | flops | bytes accessed | tf_op | source)
XLA Modules:
  0.0 124.6 jit_solution(8993275246623028613)
XLA Ops:
  0.6 110.6 %shard_map.86 = (f32[64,1024]{1,0:T(8,128)}, bf16[4,2,4,2,16,4096]{5,4,3,2,1,0:T(8,128)(2,1)}, bf16[1024,1024]{1,0:T(8,128)(2,1)}, f32[1024,1024]{1,0:T(8,128)}) custom-call(bf16[64,1024]{1,0:T(8,128)(2,1)} %hidden_ref.1, bf16[1024,4096]{1,0:T(8,128)(2,1)} %head_ref.1, bf16[128,4096]{1,0:T(8,128)(2,1)} %refs_ref.1, s32[8,128]{1,0:T(8,128)} %bitcast.6, ...), custom_call_target="tpu_custom_call" | custom-call | tf_op jit(solution)/shard_map/pallas_call | solution.py:535
  111.3 13.2 %shard_map.87 = (f32[64,1024]{1,0:T(8,128)}, f32[1024,4096]{1,0:T(8,128)}) custom-call(bf16[1024,1024]{1,0:T(8,128)(2,1)} %get-tuple-element.6.rows_ref, bf16[1024,4096]{1,0:T(8,128)(2,1)} %bitcast.5, f32[1024,1024]{1,0:T(8,128)} %get-tuple-element.8.early_ref, f32[64,1024]{1,0:T(8,128)} %get-tuple-element.9.hidden_ref), custom_call_target="tpu_custom_call" | custom-call | tf_op jit(solution)/shard_map/pallas_call | solution.py:505

commit v4 on v3

--- a/solution.py
+++ b/solution.py
@@ -483,16 +483,16 @@
         if i == 0:
             for copy in taken:
                 copy.start()
-        if i == 1:
-            for copy, last in zip(taken, passed):
-                copy.wait()
-                last.start()
         if i + 3 < len(loads):
             loads[i + 3].start()
         if i >= 2:
             stores[i - 2].wait()
         here = outs.at[i % 2, :, pl.ds(0, SPANS[i])]
         here[...] = jnp.dot(rows[...], grads[:, span], preferred_element_type=F32)
+        if i == 1:
+            for copy, last in zip(taken, passed):
+                copy.wait()
+                last.start()
         stores.append(pltpu.make_async_copy(here, out_ref.at[:, span], out_sem.at[i]))
         stores[-1].start()
     for copy in stores[-2:] + passed:

time: 125 us -> 123 us (0.984)
  Pallas kernels: 124 us -> 122 us
    pallas_call x1, Pallas kernels: 13.2 us -> 11.8 us  [head_gradient(): pl.pallas_call(head_kernel, out_shape=(jax.ShapeDtypeStruct(hidden_grad.s...]
where the time goes in v4:
time: 123 us
  Pallas kernels  122 us (99%)
    pallas_call x1, Pallas kernels, per_device(): pl.pallas_call(kernel, out_shape=(jax.ShapeDtypeStruct((CHUNKS * ROWS, de...  111 us
    pallas_call x1, Pallas kernels, head_gradient(): pl.pallas_call(head_kernel, out_shape=(jax.ShapeDtypeStruct(hidden_grad.s...  11.8 us

profile of v4, /device:TPU:1, one launch (start us, length us, event | category | flops | bytes accessed | tf_op | source)
XLA Modules:
  0.0 123.3 jit_solution(4607999928126851402)
XLA Ops:
  0.6 110.6 %shard_map.86 = (f32[64,1024]{1,0:T(8,128)}, bf16[4,2,4,2,16,4096]{5,4,3,2,1,0:T(8,128)(2,1)}, bf16[1024,1024]{1,0:T(8,128)(2,1)}, f32[1024,1024]{1,0:T(8,128)}) custom-call(bf16[64,1024]{1,0:T(8,128)(2,1)} %hidden_ref.1, bf16[1024,4096]{1,0:T(8,128)(2,1)} %head_ref.1, bf16[128,4096]{1,0:T(8,128)(2,1)} %refs_ref.1, s32[8,128]{1,0:T(8,128)} %bitcast.6, ...), custom_call_target="tpu_custom_call" | custom-call | tf_op jit(solution)/shard_map/pallas_call | solution.py:535
  111.3 11.8 %shard_map.87 = (f32[64,1024]{1,0:T(8,128)}, f32[1024,4096]{1,0:T(8,128)}) custom-call(bf16[1024,1024]{1,0:T(8,128)(2,1)} %get-tuple-element.6.rows_ref, bf16[1024,4096]{1,0:T(8,128)(2,1)} %bitcast.5, f32[1024,1024]{1,0:T(8,128)} %get-tuple-element.8.early_ref, f32[64,1024]{1,0:T(8,128)} %get-tuple-element.9.hidden_ref), custom_call_target="tpu_custom_call" | custom-call | tf_op jit(solution)/shard_map/pallas_call | solution.py:505
